TPU v7x, 256 devices: a whole 4x4x8 slice. The times are simulated.
256 devices in a mesh: fx: 32 (over z, x), fy: 8 (over y, core).
Axes of the slice: x: 4, y: 4, z: 8, core: 2. Of those that a mesh axis runs over, the one named last changes fastest.
Arguments:
- sky_image: float32 [32, 65536], P('fy', 'fx'), may hold values from -6 to 6
- col_off: int32 [32], replicated, may hold values from 0 to 65535
- row_off: int32 [8], replicated, may hold values from 0 to 65535
- layer_counts: int32 [32, 8], P('fx', 'fy'), may hold values from 1 to 8
- w_steps: int32 [32, 8, 8], P('fx', 'fy'), may hold values from 1 to 4
- live_blocks: int32 [32, 8], P('fx', 'fy'), may hold values from 1 to 16
- block_codes: int32 [32, 8, 16], P('fx', 'fy'), may hold values from 0 to 839
- vis_coords: float32 [32, 8, 16, 2, 128], P('fx', 'fy'), may hold values from 0 to 1
Outputs:
- visibilities: float32 [32, 8, 16, 2, 128], P('fx', 'fy')
All inputs are finite; a program needn't handle non-finite values.
Results may differ from a plain program's by a relative error of at most 0.018.
Values may be sent and summed in bfloat16 or wider, within the bound.
A program may use at most 64 MiB of HBM per device.

v0:
```python
import math

import jax
import jax.numpy as jnp
from jax import lax
from jax.sharding import PartitionSpec as P

SG = 1024
NSKY = 65536


two_pi = 6.283185307179586
coarse_step = 32


def mulmod(factor_a, factor_b, modulus):
    high_part = factor_b // 256
    low_part = factor_b % 256
    reduced = factor_a * high_part % modulus
    return (reduced * 256 + factor_a * low_part) % modulus


def precise(matrix_a, matrix_b):
    return jnp.dot(
        matrix_a, matrix_b, precision=lax.Precision.HIGHEST, preferred_element_type=jnp.float32
    )


def pick_offset(offsets, selector):
    slots = jnp.arange(offsets.shape[0], dtype=jnp.int32)
    chosen = jnp.sum(jnp.where(selector[:, None] == slots[None, :], offsets[None, :], 0), axis=1)
    return chosen


def build_layers(subgrid, steps_list):
    rows_grid = subgrid.shape[0]
    cols_grid = subgrid.shape[1] // 2
    depths = jnp.cumsum(steps_list)
    centre_rows = jnp.arange(rows_grid, dtype=jnp.int32) - rows_grid // 2
    centre_cols = jnp.arange(cols_grid, dtype=jnp.int32) - cols_grid // 2
    radial = (
        centre_rows[:, None] * centre_rows[:, None] + centre_cols[None, :] * centre_cols[None, :]
    )
    screen = (
        math.pi
        / cols_grid
        * (depths[:, None, None] * radial[None, :, :] % (2 * cols_grid)).astype(jnp.float32)
    )
    cosine = jnp.cos(screen)
    sine_part = jnp.sin(screen)
    grid_real = subgrid[:, :cols_grid]
    grid_imag = subgrid[:, cols_grid:]
    layer_real = grid_real[None] * cosine - grid_imag[None] * sine_part
    layer_imag = grid_real[None] * sine_part + grid_imag[None] * cosine
    return jnp.concatenate([layer_real, layer_imag], axis=1).astype(jnp.bfloat16)


def kernel_visibilities(stacked, u_pos, v_pos):
    rows_grid = stacked.shape[0] // 2
    cols_grid = stacked.shape[1]
    count_vis = v_pos.shape[0]
    coarse = (jnp.arange(cols_grid // coarse_step, dtype=jnp.int32) * coarse_step).astype(
        jnp.float32
    )
    fine_part = jnp.arange(coarse_step, dtype=jnp.int32).astype(jnp.float32)
    coarse_angle = two_pi * coarse[:, None] * v_pos[None, :]
    fine_angle = two_pi * fine_part[:, None] * v_pos[None, :]
    coarse_cos = jnp.cos(coarse_angle)[:, None, :]
    coarse_sin = jnp.sin(coarse_angle)[:, None, :]
    fine_cos = jnp.cos(fine_angle)[None, :, :]
    fine_sin = jnp.sin(fine_angle)[None, :, :]
    kernel_real = (coarse_cos * fine_cos - coarse_sin * fine_sin).reshape(cols_grid, count_vis)
    kernel_imag = (coarse_sin * fine_cos + coarse_cos * fine_sin).reshape(cols_grid, count_vis)
    kernel = jnp.concatenate([kernel_real, kernel_imag], axis=1).astype(jnp.bfloat16)
    products = jnp.dot(stacked, kernel, preferred_element_type=jnp.float32)
    part_real = products[:rows_grid, :count_vis] - products[rows_grid:, count_vis:]
    part_imag = products[:rows_grid, count_vis:] + products[rows_grid:, :count_vis]
    row_angle = (
        two_pi
        * jnp.arange(rows_grid, dtype=jnp.int32).astype(jnp.float32)[:, None]
        * u_pos[None, :]
    )
    row_cos = jnp.cos(row_angle)
    row_sin = jnp.sin(row_angle)
    vis_scale = 1.0 / math.sqrt(rows_grid * cols_grid)
    vis_real = jnp.sum(row_cos * part_real - row_sin * part_imag, axis=0) * vis_scale
    vis_imag = jnp.sum(row_cos * part_imag + row_sin * part_real, axis=0) * vis_scale
    return jnp.stack([vis_real, vis_imag])


def per_device(
    sky_image, col_off, row_off, layer_counts, w_steps, live_blocks, block_codes, vis_coords
):
    rows_here, facet_cols = sky_image.shape
    num_cols = lax.axis_size("fx")
    num_rows = lax.axis_size("fy")
    col_index = lax.axis_index("fx")
    row_index = lax.axis_index("fy")
    total_cols = facet_cols * num_cols
    total_rows = rows_here * num_rows
    block_width = min(facet_cols, 128)
    col_phase = -two_pi / total_cols
    col_scale = 1.0 / math.sqrt(total_cols)
    band_cols = jnp.arange(SG, dtype=jnp.int32)

    def one_turn(carry, turn_index):
        acc_real, acc_imag = carry
        local_cols = turn_index * block_width + jnp.arange(block_width, dtype=jnp.int32)
        pieces = lax.dynamic_slice_in_dim(sky_image, turn_index * block_width, block_width, 1)
        pre_angle = col_phase * (local_cols[None, :] * col_off[:, None] % total_cols).astype(
            jnp.float32
        )
        pre_real = (jnp.cos(pre_angle)[:, None, :] * pieces[None, :, :]).reshape(
            num_cols * rows_here, block_width
        )
        pre_imag = (jnp.sin(pre_angle)[:, None, :] * pieces[None, :, :]).reshape(
            num_cols * rows_here, block_width
        )
        table_angle = col_phase * (local_cols[:, None] * band_cols[None, :] % total_cols).astype(
            jnp.float32
        )
        table_real = jnp.cos(table_angle)
        table_imag = jnp.sin(table_angle)
        acc_real = acc_real + precise(pre_real, table_real) - precise(pre_imag, table_imag)
        acc_imag = acc_imag + precise(pre_real, table_imag) + precise(pre_imag, table_real)
        return ((acc_real, acc_imag), None)

    zeros_acc = jnp.zeros((num_cols * rows_here, SG), jnp.float32)
    turn_list = jnp.arange(facet_cols // block_width, dtype=jnp.int32)
    (sum_real, sum_imag), unused = lax.scan(one_turn, (zeros_acc, zeros_acc), turn_list)
    wave_cols = (col_off[:, None] + band_cols[None, :]) % total_cols
    turned = mulmod(col_index * facet_cols % total_cols, wave_cols, total_cols)
    post_angle = col_phase * turned.astype(jnp.float32)
    post_cos = jnp.cos(post_angle)[:, None, :]
    post_sin = jnp.sin(post_angle)[:, None, :]
    sum_real = sum_real.reshape(num_cols, rows_here, SG)
    sum_imag = sum_imag.reshape(num_cols, rows_here, SG)
    band_real = (sum_real * post_cos - sum_imag * post_sin) * col_scale
    band_imag = (sum_real * post_sin + sum_imag * post_cos) * col_scale
    band_data = jnp.stack([band_real, band_imag], axis=2)
    received = lax.all_to_all(
        band_data.astype(jnp.bfloat16), "fx", split_axis=0, concat_axis=0, tiled=True
    )
    strips = jnp.sum(received.astype(jnp.float32), axis=0)
    strips = strips.astype(jnp.bfloat16)
    row_phase = -two_pi / NSKY
    row_scale = 1.0 / math.sqrt(total_rows)
    facet_stride = NSKY // num_rows
    strip_real = strips[:, 0, :].astype(jnp.float32)
    strip_imag = strips[:, 1, :].astype(jnp.float32)
    own_cells = row_index * facet_stride + jnp.arange(rows_here, dtype=jnp.int32)
    index_rows = jnp.arange(lax.axis_size("fy") * total_rows, dtype=jnp.int32)
    wave_rows = (pick_offset(row_off, index_rows // total_rows) + index_rows % total_rows) % NSKY
    angles = row_phase * mulmod(own_cells[None, :], wave_rows[:, None], NSKY).astype(jnp.float32)
    tab_cos = jnp.cos(angles)
    tab_sin = jnp.sin(angles)
    term_real = (precise(tab_cos, strip_real) - precise(tab_sin, strip_imag)) * row_scale
    term_imag = (precise(tab_cos, strip_imag) + precise(tab_sin, strip_real)) * row_scale
    subgrid = lax.psum_scatter(
        jnp.concatenate([term_real, term_imag], axis=1).astype(jnp.bfloat16),
        "fy",
        scatter_dimension=0,
        tiled=True,
    ).astype(jnp.float32)
    layers = build_layers(subgrid, w_steps[0, 0, :])
    count_here = layer_counts[0, 0]
    codes_here = block_codes[0, 0]
    coords_here = vis_coords[0, 0]

    def degrid(block_index, buffer):
        plane_index = (
            lax.dynamic_index_in_dim(codes_here, block_index, 0, keepdims=False) % count_here
        )
        stacked = lax.dynamic_index_in_dim(layers, plane_index, 0, keepdims=False)
        coords = lax.dynamic_index_in_dim(coords_here, block_index, 0, keepdims=False)
        values = kernel_visibilities(stacked, coords[0], coords[1])
        return lax.dynamic_update_index_in_dim(buffer, values, block_index, 0)

    initial = jnp.zeros(coords_here.shape, jnp.float32)
    result = lax.fori_loop(0, live_blocks[0, 0], degrid, initial)
    return result[None, None]


def solution(mesh):
    placed = (
        P("fy", "fx"),
        P(),
        P(),
        P("fx", "fy"),
        P("fx", "fy", None),
        P("fx", "fy"),
        P("fx", "fy", None),
        P("fx", "fy", None, None, None),
    )
    return jax.shard_map(
        per_device,
        mesh=mesh,
        in_specs=placed,
        out_specs=P("fx", "fy", None, None, None),
        check_vma=False,
    )
```

profile of v0, /device:TPU:33, one launch (start us, length us, event | category | flops | bytes accessed | tf_op | source)
XLA Modules:
  0.0 355.1 jit_solution(8619962146252362566)
XLA Ops:
  6.5 212.1 %while.28 = (s32[]{:T(128)}, f32[128,1024]{1,0:T(8,128)S(1)}, f32[128,1024]{1,0:T(8,128)S(1)}, s32[16]{0:T(128)S(1)}, s32[32]{0:T(128)}, /*index=5*/f32[4,2048]{...) while((s32[]{:T(128)}, f32[128,1024]{1,0:T(8,128)S(1)}, f32[128,1024]{1,0:T(8,128)S(1)}, ...), condition=%wide.region_2.3_spmd.clone, body=%wide.region_1.2_spmd.clone.sunk | while | flops 813523072 | bytes 4662586 | solution.py:130
  14.6 2.6 convolution_add_fusion.8
  27.9 2.6 convolution_add_fusion.8
  38.5 2.6 convolution_subtract_fusion.3
  41.1 2.6 convolution_add_fusion.8
  54.3 2.6 convolution_add_fusion.8
  67.6 2.6 convolution_add_fusion.8
  80.8 2.6 convolution_add_fusion.8
  94.1 2.6 convolution_add_fusion.8
  104.8 2.6 convolution_subtract_fusion.3
  107.3 2.6 convolution_add_fusion.8
  120.6 2.6 convolution_add_fusion.8
  133.8 2.6 convolution_add_fusion.8
  147.1 2.6 convolution_add_fusion.8
  160.3 2.6 convolution_add_fusion.8
  173.6 2.6 convolution_add_fusion.8
  186.8 2.6 convolution_add_fusion.8
  200.1 2.6 convolution_add_fusion.8
  213.3 2.6 convolution_add_fusion.8
  221.7 10.6 %all-to-all-start = ((bf16[32,4,2,1024]{3,1,2,0:T(4,128)(2,1)}), bf16[32,4,2,1024]{3,1,2,0:T(4,128)(2,1)S(1)}, u32[]{:S(2)}, u32[]{:S(2)}) async-start(bf16[32,4,2,1024]{3,1,2,0:T(4,128)(2,1)} %pad_maximum_fusion.2), calls=%async_computation | async-start | bytes 1048576 | tf_op jit(solution)/shard_map/all_to_all | solution.py:141
  232.5 15.0 %all-to-all-done = bf16[32,4,2,1024]{3,1,2,0:T(4,128)(2,1)S(1)} async-done(((bf16[32,4,2,1024]{3,1,2,0:T(4,128)(2,1)}), bf16[32,4,2,1024]{3,1,2,0:T(4,128)(2,1)S(1)}, u32[]{:S(2)}, u32[]{:S(2)}) %all-to-all-start) | async-done | bytes 524320 | tf_op jit(solution)/shard_map/all_to_all | solution.py:141
  254.4 30.1 %reduce-scatter.2.cloned.1.call-done = bf16[32,2048]{1,0:T(8,128)(2,1)} async-done(((bf16[256,2048]{1,0:T(8,128)(2,1)}), bf16[32,2048]{1,0:T(8,128)(2,1)}) %reduce-scatter.2.cloned.1.call-update) | async-done | bytes 131088 | tf_op jit(solution)/shard_map/reduce_scatter | solution.py:159
  285.4 4.5 %subtract_convert_fusion.1 = (bf16[8,32,1024]{2,1,0:T(8,128)(2,1)S(1)}, bf16[8,32,1024]{2,1,0:T(8,128)(2,1)S(1)}) fusion(f32[32,1024]{1,0:T(8,128)S(1)} %get-tuple-element.267, s32[32,1024]{1,0:T(8,128)S(1)} %broadcast_add_fusion, s32[8]{0:T(128)S(1)} %bitcast.79, f32[32,1024]{1,0:T(8,128)S(1)} %get-tuple-element.266), kind=kLoop, calls=%fused_computation.99 | loop fusion | flops 5767168 | bytes 1441824 | tf_op jit(solution)/shard_map/convert.5
  290.6 57.1 %while.27 = (s32[]{:T(128)}, f32[16,2,128]{2,1,0:T(2,128)S(1)}, s32[]{:T(128)}, f32[16,2,128]{2,1,0:T(2,128)}, s32[16]{0:T(128)S(1)}, /*index=5*/s32[]{:T(128)},...) while((s32[]{:T(128)}, f32[16,2,128]{2,1,0:T(2,128)S(1)}, ...), condition=%wide.region_9.10_spmd, body=%wide.region_6.9_spmd.sunk | while | flops 35705264 | bytes 1452950 | solution.py:180
  (340 shorter events, 198.1 us)
Async XLA Ops:
  218.7 0.7 copy-start
  220.5 11.9 %copy-start.2 = (s32[8]{0:T(128)S(1)}, s32[8]{0:T(128)}, u32[]{:S(2)}) copy-start(s32[8]{0:T(128)} %param.14) | copy-start | bytes 100
  221.7 25.9 %all-to-all-start = ((bf16[32,4,2,1024]{3,1,2,0:T(4,128)(2,1)}), bf16[32,4,2,1024]{3,1,2,0:T(4,128)(2,1)S(1)}, u32[]{:S(2)}, u32[]{:S(2)}) async-start(bf16[32,4,2,1024]{3,1,2,0:T(4,128)(2,1)} %pad_maximum_fusion.2), calls=%async_computation | async-start | bytes 1048576 | tf_op jit(solution)/shard_map/all_to_all | solution.py:141
  232.3 52.2 %reduce-scatter.2.cloned.1.call-start = ((), (), s32[]{:S(2)}) async-start(), calls=%async_computation.2 | async-start | bytes 1179648 | tf_op jit(solution)/shard_map/reduce_scatter | solution.py:159
  253.5 0.7 copy-start.3
  289.9 0.7 copy-start.4
  347.6 0.6 copy-start.1
Sparse Core Ops, SparseCore 0:
  253.6 30.8 reduce-scatter.1
where the time goes:
time: 359 us; the launch traced here: 355 us
  matrix products  172 us (48%)
  local copies, waits for them, and re-layouts  46.1 us (13%)
  waiting for transfers between devices  45.1 us (13%)
  loops' own time  35.9 us (10%)
  other arithmetic  30.6 us (9%)
  between operations  14.2 us (4%)
  starting transfers between devices  10.7 us (3%)
    dot_general x68, matrix products, precise(): jnp.dot(matrix_a, matrix_b, precision=lax.Precision.HIGHEST, preferred_el...  169 us
    reduce_scatter x1, waiting for transfers between devices, per_device(): lax.psum_scatter(jnp.concatenate([term_real, term_imag], axis=1).astype(j...  30.1 us
    another operation x1, loops' own time, per_device(): result = lax.fori_loop(0, live_blocks[0, 0], degrid, initial)  23.4 us
    all_to_all x1, waiting for transfers between devices, per_device(): lax.all_to_all(band_data.astype(jnp.bfloat16), 'fx', split_axis=0, concat...  15 us
    sin x16, other arithmetic, one_turn(): jnp.sin(pre_angle)[:, None, :] * pieces[None, :, :]  12.9 us
    another operation x1, loops' own time, per_device(): lax.scan(one_turn, (zeros_acc, zeros_acc), turn_list)  12.5 us
    dynamic_slice x16, local copies, waits for them, and re-layouts, one_turn(): lax.dynamic_slice_in_dim(sky_image, turn_index * block_width, block_width...  11 us
    dynamic_slice x16, local copies, waits for them, and re-layouts, degrid(): lax.dynamic_index_in_dim(coords_here, block_index, 0, keepdims=False)  10.9 us
  transfers between devices with their start and end apart: 2, of which 2 were waited for; matrix products, arithmetic and copies ran while one was open for 0% of the time, Pallas kernels for 0%

commit v1 on v0

--- a/solution.py
+++ b/solution.py
@@ -35,7 +35,8 @@
 def build_layers(subgrid, steps_list):
     rows_grid = subgrid.shape[0]
     cols_grid = subgrid.shape[1] // 2
-    depths = jnp.cumsum(steps_list)
+    slots = jnp.arange(steps_list.shape[0], dtype=jnp.int32)
+    depths = jnp.sum(jnp.where(slots[None, :] <= slots[:, None], steps_list[None, :], 0), axis=1)
     centre_rows = jnp.arange(rows_grid, dtype=jnp.int32) - rows_grid // 2
     centre_cols = jnp.arange(cols_grid, dtype=jnp.int32) - cols_grid // 2
     radial = (

time: 359 us -> 360 us (level)
  the two profiles are of different devices: /device:TPU:33 before, /device:TPU:6 now
where the time goes in v1:
time: 360 us; the launch traced here: 358 us
  matrix products  172 us (48%)
  waiting for transfers between devices  47.3 us (13%)
  local copies, waits for them, and re-layouts  46.1 us (13%)
  loops' own time  35.9 us (10%)
  other arithmetic  30.6 us (8%)
  between operations  14.3 us (4%)
  starting transfers between devices  11.6 us (3%)
    dot_general x68, matrix products, precise(): jnp.dot(matrix_a, matrix_b, precision=lax.Precision.HIGHEST, preferred_el...  169 us
    reduce_scatter x1, waiting for transfers between devices, per_device(): lax.psum_scatter(jnp.concatenate([term_real, term_imag], axis=1).astype(j...  30.7 us
    another operation x1, loops' own time, per_device(): result = lax.fori_loop(0, live_blocks[0, 0], degrid, initial)  23.4 us
    all_to_all x1, waiting for transfers between devices, per_device(): lax.all_to_all(band_data.astype(jnp.bfloat16), 'fx', split_axis=0, concat...  16.6 us
    sin x16, other arithmetic, one_turn(): jnp.sin(pre_angle)[:, None, :] * pieces[None, :, :]  12.9 us
    another operation x1, loops' own time, per_device(): lax.scan(one_turn, (zeros_acc, zeros_acc), turn_list)  12.5 us
    all_to_all x1, starting transfers between devices, per_device(): lax.all_to_all(band_data.astype(jnp.bfloat16), 'fx', split_axis=0, concat...  11.6 us
    dynamic_slice x16, local copies, waits for them, and re-layouts, one_turn(): lax.dynamic_slice_in_dim(sky_image, turn_index * block_width, block_width...  11 us
  transfers between devices with their start and end apart: 2, of which 2 were waited for; matrix products, arithmetic and copies ran while one was open for 0% of the time, Pallas kernels for 0%

profile of v1, /device:TPU:6, one launch (start us, length us, event | category | flops | bytes accessed | tf_op | source)
XLA Modules:
  0.0 358.1 jit_solution(9189238580509690224)
XLA Ops:
  6.5 212.1 %while.28 = (s32[]{:T(128)}, f32[128,1024]{1,0:T(8,128)S(1)}, f32[128,1024]{1,0:T(8,128)S(1)}, s32[16]{0:T(128)S(1)}, s32[32]{0:T(128)}, /*index=5*/f32[4,2048]{...) while((s32[]{:T(128)}, f32[128,1024]{1,0:T(8,128)S(1)}, f32[128,1024]{1,0:T(8,128)S(1)}, ...), condition=%wide.region_2.3_spmd.clone, body=%wide.region_1.2_spmd.clone.sunk | while | flops 813523072 | bytes 4662586 | solution.py:131
  14.6 2.6 convolution_add_fusion.8
  27.9 2.6 convolution_add_fusion.8
  38.5 2.6 convolution_subtract_fusion.3
  41.1 2.6 convolution_add_fusion.8
  54.3 2.6 convolution_add_fusion.8
  67.6 2.6 convolution_add_fusion.8
  78.3 2.6 convolution_subtract_fusion.3
  80.8 2.6 convolution_add_fusion.8
  94.1 2.6 convolution_add_fusion.8
  107.3 2.6 convolution_add_fusion.8
  120.6 2.6 convolution_add_fusion.8
  133.8 2.6 convolution_add_fusion.8
  147.1 2.6 convolution_add_fusion.8
  160.3 2.6 convolution_add_fusion.8
  173.6 2.6 convolution_add_fusion.8
  186.8 2.6 convolution_add_fusion.8
  200.1 2.6 convolution_add_fusion.8
  213.3 2.6 convolution_add_fusion.8
  221.7 11.6 %all-to-all-start = ((bf16[32,4,2,1024]{3,1,2,0:T(4,128)(2,1)}), bf16[32,4,2,1024]{3,1,2,0:T(4,128)(2,1)S(1)}, u32[]{:S(2)}, u32[]{:S(2)}) async-start(bf16[32,4,2,1024]{3,1,2,0:T(4,128)(2,1)} %pad_maximum_fusion.2), calls=%async_computation | async-start | bytes 1048576 | tf_op jit(solution)/shard_map/all_to_all | solution.py:142
  233.5 16.6 %all-to-all-done = bf16[32,4,2,1024]{3,1,2,0:T(4,128)(2,1)S(1)} async-done(((bf16[32,4,2,1024]{3,1,2,0:T(4,128)(2,1)}), bf16[32,4,2,1024]{3,1,2,0:T(4,128)(2,1)S(1)}, u32[]{:S(2)}, u32[]{:S(2)}) %all-to-all-start) | async-done | bytes 524320 | tf_op jit(solution)/shard_map/all_to_all | solution.py:142
  256.9 30.7 %reduce-scatter.2.cloned.1.call-done = bf16[32,2048]{1,0:T(8,128)(2,1)} async-done(((bf16[256,2048]{1,0:T(8,128)(2,1)}), bf16[32,2048]{1,0:T(8,128)(2,1)}) %reduce-scatter.2.cloned.1.call-update) | async-done | bytes 131088 | tf_op jit(solution)/shard_map/reduce_scatter | solution.py:160
  288.4 4.5 %subtract_convert_fusion.1 = (bf16[8,32,1024]{2,1,0:T(8,128)(2,1)S(1)}, bf16[8,32,1024]{2,1,0:T(8,128)(2,1)S(1)}) fusion(f32[32,1024]{1,0:T(8,128)S(1)} %get-tuple-element.267, s32[32,1024]{1,0:T(8,128)S(1)} %broadcast_add_fusion, s32[8]{0:T(128)S(1)} %select_reduce_fusion.1, f32[32,1024]{1,0:T(8,128)S(1)} %get-tuple-element.266), kind=kLoop, calls=%fused_computation.99 | loop fusion | flops 5767168 | bytes 1441824 | tf_op jit(solution)/shard_map/convert.5
  293.6 57.1 %while.27 = (s32[]{:T(128)}, f32[16,2,128]{2,1,0:T(2,128)S(1)}, s32[]{:T(128)}, f32[16,2,128]{2,1,0:T(2,128)}, s32[16]{0:T(128)S(1)}, /*index=5*/s32[]{:T(128)},...) while((s32[]{:T(128)}, f32[16,2,128]{2,1,0:T(2,128)S(1)}, ...), condition=%wide.region_9.10_spmd, body=%wide.region_6.9_spmd.sunk | while | flops 35705264 | bytes 1452950 | solution.py:181
  (340 shorter events, 198.0 us)
Async XLA Ops:
  218.7 0.7 copy-start
  220.5 12.8 %copy-start.2 = (s32[8]{0:T(128)S(1)}, s32[8]{0:T(128)}, u32[]{:S(2)}) copy-start(s32[8]{0:T(128)} %param.14) | copy-start | bytes 100
  221.7 28.4 %all-to-all-start = ((bf16[32,4,2,1024]{3,1,2,0:T(4,128)(2,1)}), bf16[32,4,2,1024]{3,1,2,0:T(4,128)(2,1)S(1)}, u32[]{:S(2)}, u32[]{:S(2)}) async-start(bf16[32,4,2,1024]{3,1,2,0:T(4,128)(2,1)} %pad_maximum_fusion.2), calls=%async_computation | async-start | bytes 1048576 | tf_op jit(solution)/shard_map/all_to_all | solution.py:142
  233.3 54.3 %reduce-scatter.2.cloned.1.call-start = ((), (), s32[]{:S(2)}) async-start(), calls=%async_computation.2 | async-start | bytes 1179648 | tf_op jit(solution)/shard_map/reduce_scatter | solution.py:160
  256.0 0.7 copy-start.3
  293.0 0.7 copy-start.4
  350.7 0.6 copy-start.1
Sparse Core Ops, SparseCore 0:
  256.1 31.3 reduce-scatter.1

commit v2 on v0

v2 whole, which is shorter than its diff:
```python
import functools

import jax
import jax.numpy as jnp
import numpy as np
from jax import lax
from jax.experimental import pallas as pl
from jax.experimental.pallas import tpu as pltpu
from jax.sharding import PartitionSpec as P

MESH = pl.DeviceIdType.MESH
SG = 1024
NSKY = 65536
NB = 16
NV = 128
SG0 = 32
NX = 4
NZ = 8
NQ = 8
HALF = SG // 2
F32 = jnp.float32
BF16 = jnp.bfloat16
SIN = (3.141592502593994, -5.167698860168457, 2.5499982833862305, -0.59855055809021, 0.0807478204369545, -0.00608947454020381)
COS = (1.0, -4.93480110168457, 4.058694839477539, -1.3351584672927856, 0.23502980172634125, -0.025358984246850014, 0.0015939107397571206)


def cis(turns):
    near = turns - jnp.floor(turns + 0.5)
    y = near + near
    z = y * y
    sine = jnp.full_like(z, SIN[-1])
    for c in SIN[-2::-1]:
        sine = sine * z + c
    cosine = jnp.full_like(z, COS[-1])
    for c in COS[-2::-1]:
        cosine = cosine * z + c
    return cosine, sine * y


def dft_table():
    row = np.arange(NZ * 32)
    b = 128 * (row // 32) + 2 * (row % 16) + (row // 16) % 2
    angle = (b[:, None] * np.arange(SG)[None, :]) % SG * (2 * np.pi / SG)
    return np.concatenate([np.cos(angle), -np.sin(angle)], axis=1).astype(BF16)


def iota(shape, axis):
    return lax.broadcasted_iota(jnp.int32, shape, axis)


def kernel(
    sky_h, col_h, row_h, cnt_h, ws_h, live_h, codes_h, crd_h, tab_h, out,
    sky, tmp, tab, crd, col, rows, cnt, ws, live, codes, gath, spec, w8, tw, ybuf, part, got, strips, ker, vtab,
    load_sem, send1, recv1, send2, recv2, send3, recv3,
):
    fx, fy = lax.axis_index("fx"), lax.axis_index("fy")
    z, x = fx // NX, lax.rem(fx, NX)

    pairs = [(sky_h, sky), (col_h, col), (row_h, rows), (cnt_h, cnt), (ws_h, ws), (live_h, live), (codes_h, codes), (crd_h, crd), (tab_h, tab)]
    loads = [pltpu.make_async_copy(a, b, load_sem.at[i]) for i, (a, b) in enumerate(pairs)]
    for load in loads:
        load.start()

    along_z = [(lax.rem(z + d, NZ) * NX + x, fy) for d in range(1, NZ)]
    along_x = [(z * NX + lax.rem(x + d, NX), fy) for d in range(1, NX)]
    along_q = [(fx, lax.rem(fy + d, NQ)) for d in range(1, NQ)]
    barrier = pltpu.get_barrier_semaphore()
    for peer in along_z + along_x + along_q:
        pl.semaphore_signal(barrier, inc=1, device_id=peer, device_id_type=MESH)

    loads[0].wait()
    for j in range(16):
        tmp[4 * j : 4 * j + 4, :] = sky[:, 128 * j : 128 * j + 128]
    left = iota((16, 128), 1) < 64
    line = [tmp[pl.ds(i, 16, stride=4), :] for i in range(4)]
    turned = [pltpu.roll(a, 64, 1) for a in line]
    halves = []
    for i in (0, 2):
        low = jnp.where(left, line[i], turned[i + 1])
        high = jnp.where(left, turned[i], line[i + 1])
        halves.append(jnp.concatenate([low, high], axis=0))
    gath[z] = jnp.concatenate(halves, axis=1).astype(BF16)

    pl.semaphore_wait(barrier, len(along_z) + len(along_x) + len(along_q))

    def phase1(d, slot):
        return pltpu.make_async_remote_copy(
            src_ref=gath.at[slot], dst_ref=gath.at[slot], send_sem=send1.at[d], recv_sem=recv1.at[d],
            device_id=along_z[d - 1], device_id_type=MESH,
        )

    sent1 = [phase1(d, z) for d in (4, 3, 5, 2, 6, 1, 7)]
    for copy in sent1:
        copy.start()
    for load in loads[1:]:
        load.wait()

    kappa = iota((8, SG), 1)
    c0 = iota((8, SG), 0)

    def wave(off):
        return off + jnp.bitwise_and(kappa - off, SG - 1)

    for d in range(NX):
        k = wave(col[z * NX + lax.rem(x + d, NX)])
        cosine, sine = cis(jnp.bitwise_and(k * 8, NSKY - 1).astype(F32) * (1.0 / NSKY))
        w8[d, 0] = cosine
        w8[d, 1] = -sine
        cosine, sine = cis(jnp.bitwise_and(c0 * k + 2048 * x * kappa, NSKY - 1).astype(F32) * (1.0 / NSKY))
        tw[d, 0] = cosine
        tw[d, 1] = -sine

    r = iota((128, 64), 0)
    m = iota((128, 64), 1)
    q, ri, i = jnp.bitwise_and(r, 63) // 8, jnp.bitwise_and(r, 7) // 4, jnp.bitwise_and(r, 3)
    turn = jnp.bitwise_and((q * (NSKY // NQ) + i) * (rows[fy] + jnp.bitwise_and(m, 31)), NSKY - 1)
    quarter = ri - (r >= 64).astype(jnp.int32) + (m >= 32).astype(jnp.int32)
    wide = cis(quarter.astype(F32) * 0.25 - turn.astype(F32) * (1.0 / NSKY))[0].astype(BF16)

    count = cnt[0, 0]
    g = iota((32, NV), 0)
    centre = g - 512
    middle = g - 16

    def tables(b):
        plane = lax.rem(codes[0, 0, b], count)
        depth = jnp.int32(0)
        for layer in range(8):
            depth = depth + jnp.where(layer <= plane, ws[0, 0, layer], 0)
        u = crd[0, 0, b, 0:1, :]
        v = crd[0, 0, b, 1:2, :]
        screen = jnp.bitwise_and(depth * middle * middle, 2047).astype(F32) * (1.0 / 2048)
        wave_real, wave_imag = cis(g.astype(F32) * u + screen)
        both = jnp.concatenate([wave_real, wave_imag], axis=0).astype(BF16)
        vtab[b] = jnp.dot(wide, both, preferred_element_type=F32)
        screen = jnp.bitwise_and(depth * centre * centre, 2047).astype(F32) * (1.0 / 2048)
        real, imag = cis(g.astype(F32) * v + screen)
        step = jnp.bitwise_and(depth * (g + 16), 31).astype(F32) * (1.0 / 32)
        step_real, step_imag = cis(32.0 * v + step)
        return real, imag, step_real, step_imag

    def fill(b2, carry):
        blocks = [2 * b2, 2 * b2 + 1]
        state = [tables(b) for b in blocks]
        fixed = [s[2:] for s in state]

        def stride(h, values):
            result = []
            for b, (real, imag), (sr, si) in zip(blocks, values, fixed):
                at = pl.ds(pl.multiple_of(32 * h, 32), 32)
                ker[b, at, 0:NV] = real.astype(BF16)
                ker[b, at, NV : 2 * NV] = imag.astype(BF16)
                result.append((real * sr - imag * si, real * si + imag * sr))
            return tuple(result)

        lax.fori_loop(0, 32, stride, tuple(s[:2] for s in state), unroll=4)
        return carry

    lax.fori_loop(0, NB // 2, fill, 0)

    for d in range(1, NZ):
        phase1(d, lax.rem(z + NZ - d, NZ)).wait_recv()

    sky_t = gath[...].reshape(NZ * 32, 256)
    spec[...] = lax.dot_general(sky_t, tab[...], (((0,), (0,)), ((), ())), preferred_element_type=F32)
    pick_row = iota((8, 64), 0)
    pick_col = iota((8, 64), 1)
    pick = jnp.where(
        (pick_col // 16 == jnp.bitwise_and(pick_row, 3)) & (jnp.bitwise_and(pick_col // 8, 1) == pick_row // 4), 1.0, 0.0
    ).astype(BF16)

    def phase2(d):
        return pltpu.make_async_remote_copy(
            src_ref=part.at[d], dst_ref=got.at[d], send_sem=send2.at[d], recv_sem=recv2.at[d],
            device_id=along_x[d - 1], device_id_type=MESH,
        )

    own = None
    for d in (2, 1, 3, 0):
        def facet_row(x0, carry):
            for lo in (0, HALF):
                cols = slice(lo, lo + HALF)
                wr, wi = w8[d, 0, :, cols], w8[d, 1, :, cols]

                def at(c1, plus):
                    return spec[pl.ds(pl.multiple_of(x0 * 64 + 8 * c1, 8), 8), lo + plus : lo + plus + HALF]

                ar, ai = at(7, 0), at(7, SG)
                for c1 in range(6, -1, -1):
                    ar, ai = ar * wr - ai * wi + at(c1, 0), ar * wi + ai * wr + at(c1, SG)
                tr, ti = tw[d, 0, :, cols], tw[d, 1, :, cols]
                both = jnp.concatenate([ar * tr - ai * ti, ar * ti + ai * tr], axis=0)
                ybuf[d, pl.ds(pl.multiple_of(x0 * 16, 16), 16), cols] = both.astype(BF16)
            return carry

        lax.fori_loop(0, 4, facet_row, 0)
        strip = jnp.dot(pick, ybuf[d], preferred_element_type=F32)
        packed = jnp.concatenate([strip[:, :HALF], strip[:, HALF:]], axis=0)
        if d:
            part[d] = packed.astype(BF16)
            phase2(d).start()
        else:
            own = packed
    for d in (1, 3, 2):
        phase2(d).wait_recv()
        own = own + got[d].astype(F32)

    flat = jnp.concatenate([own[:8], own[8:]], axis=1)
    flat = pltpu.roll(flat, jnp.bitwise_and(SG - jnp.bitwise_and(col[fx], SG - 1), SG - 1), 1)
    strips[fy] = jnp.concatenate([flat[:, :HALF], flat[:, HALF:]], axis=0).astype(BF16)

    def phase3(d, slot):
        return pltpu.make_async_remote_copy(
            src_ref=strips.at[slot], dst_ref=strips.at[slot], send_sem=send3.at[d], recv_sem=recv3.at[d],
            device_id=along_q[d - 1], device_id_type=MESH,
        )

    sent3 = [phase3(d, fy) for d in (4, 3, 5, 2, 6, 1, 7)]
    for copy in sent3:
        copy.start()
    for d in range(1, NQ):
        phase3(d, lax.rem(fy + NQ - d, NQ)).wait_recv()
    wide_strips = strips[...].astype(F32)
    left_half = wide_strips[:, 0:8, :].reshape(64, HALF)
    right_half = wide_strips[:, 8:16, :].reshape(64, HALF)
    lines = jnp.concatenate([left_half, right_half], axis=1).astype(BF16)

    def degrid(b, carry):
        prod = jnp.dot(lines, ker[b], preferred_element_type=F32)
        vr, vi = vtab[b, 0:64, :], vtab[b, 64:128, :]
        pr, pi = prod[:, :NV], prod[:, NV:]
        scale = jnp.where(b < live[0, 0], 2.0**-18, 0.0)
        out[0, 0, b, 0:1, :] = jnp.sum(vr * pr - vi * pi, axis=0, keepdims=True) * scale
        out[0, 0, b, 1:2, :] = jnp.sum(vr * pi + vi * pr, axis=0, keepdims=True) * scale
        return carry

    lax.fori_loop(0, NB, degrid, 0, unroll=4)

    for copy in sent1:
        copy.wait_send()
    for d in (2, 1, 3):
        phase2(d).wait_send()
    for copy in sent3:
        copy.wait_send()


def per_device(sky, col, rows, cnt, ws, live, codes, crd):
    hbm = pl.BlockSpec(memory_space=pl.ANY)
    dma = pltpu.SemaphoreType.DMA
    return pl.pallas_call(
        kernel,
        out_shape=jax.ShapeDtypeStruct((1, 1, NB, 2, NV), F32),
        in_specs=[hbm] * 9,
        out_specs=pl.BlockSpec(memory_space=pltpu.VMEM),
        scratch_shapes=[
            pltpu.VMEM((4, 2048), F32),
            pltpu.VMEM((64, 128), F32),
            pltpu.VMEM((256, 2 * SG), BF16),
            pltpu.VMEM((1, 1, NB, 2, NV), F32),
            pltpu.SMEM((32,), jnp.int32),
            pltpu.SMEM((8,), jnp.int32),
            pltpu.SMEM((1, 1), jnp.int32),
            pltpu.SMEM((1, 1, 8), jnp.int32),
            pltpu.SMEM((1, 1), jnp.int32),
            pltpu.SMEM((1, 1, NB), jnp.int32),
            pltpu.VMEM((NZ, 32, 256), BF16),
            pltpu.VMEM((256, 2 * SG), F32),
            pltpu.VMEM((NX, 2, 8, SG), F32),
            pltpu.VMEM((NX, 2, 8, SG), F32),
            pltpu.VMEM((NX, 64, SG), BF16),
            pltpu.VMEM((NX, 16, HALF), BF16),
            pltpu.VMEM((NX, 16, HALF), BF16),
            pltpu.VMEM((NQ, 16, HALF), BF16),
            pltpu.VMEM((NB, SG, 2 * NV), BF16),
            pltpu.VMEM((NB, 128, NV), F32),
            dma((9,)), dma((NZ,)), dma((NZ,)), dma((NX,)), dma((NX,)), dma((NQ,)), dma((NQ,)),
        ],
        compiler_params=pltpu.CompilerParams(collective_id=0, has_side_effects=True, vmem_limit_bytes=60 * 2**20),
    )(sky, col, rows, cnt, ws, live, codes, crd, jnp.asarray(dft_table()))


def solution(mesh):
    placed = (
        P("fy", "fx"), P(), P(), P("fx", "fy"), P("fx", "fy", None), P("fx", "fy"), P("fx", "fy", None),
        P("fx", "fy", None, None, None),
    )
    return jax.shard_map(
        per_device, mesh=mesh, in_specs=placed, out_specs=P("fx", "fy", None, None, None), check_vma=False
    )
```

time: 359 us -> 30.8 us (0.09)
  the two profiles are of different devices: /device:TPU:33 before, /device:TPU:1 now
where the time goes in v2:
time: 30.8 us; the launch traced here: 30.7 us
  Pallas kernels  28 us (91%)
  local copies, waits for them, and re-layouts  1.32 us (4%)
  between operations  1.3 us (4%)
    pallas_call x1, Pallas kernels, per_device(): pl.pallas_call(kernel, out_shape=jax.ShapeDtypeStruct((1, 1, NB, 2, NV),...  28 us
    unnamed x1, local copies, waits for them, and re-layouts  1.32 us

profile of v2, /device:TPU:1, one launch (start us, length us, event | category | flops | bytes accessed | tf_op | source)
XLA Modules:
  0.0 30.7 jit_solution(5594510192495185199)
XLA Ops:
  1.3 28.0 %shard_map.91 = f32[1,1,16,2,128]{4,3,2,1,0:T(2,128)} custom-call(f32[4,2048]{1,0:T(4,128)} %sky_h.1, s32[32]{0:T(128)} %col_h.1, s32[8]{0:T(128)} %row_h.1, s32[1,1]{1,0:T(1,128)S(6)} %copy.11.cnt_h, s32[1,1,8]{2,1,0:T(1,128)} %ws_h.1, s32[1,1]{1,0:T(1,128)S(6)} %copy.12.live_h, s32[1,1,16]{2,1,0:T(1,128)} %codes_h.1, f32[1,1,16,2,128]{4,3,2,1,0:T(2,128)} %crd_h.1, ...), custom_call_target="tpu_custom_call" | custom-call | tf_op jit(solution)/shard_map/pallas_call | solution.py:250
  29.3 1.3 %copy.13 = f32[1,1,16,2,128]{4,3,2,1,0:T(2,128)} copy(f32[1,1,16,2,128]{4,3,2,1,0:T(2,128)} %shard_map.91) | data formatting | bytes 32768

commit v3 on v2

--- a/solution.py
+++ b/solution.py
@@ -50,23 +50,23 @@
 
 def kernel(
     sky_h, col_h, row_h, cnt_h, ws_h, live_h, codes_h, crd_h, tab_h, out,
-    sky, tmp, tab, crd, col, rows, cnt, ws, live, codes, gath, spec, w8, tw, ybuf, part, got, strips, ker, vtab,
+    sky, tmp, tab, crd, col, rows, cnt, ws, live, codes, gath, spec, w8, tw, ybuf, part, got, strips, cross, lines, fine, vtab, wtab, form,
     load_sem, send1, recv1, send2, recv2, send3, recv3,
 ):
     fx, fy = lax.axis_index("fx"), lax.axis_index("fy")
     z, x = fx // NX, lax.rem(fx, NX)
 
+    along_z = [(lax.rem(z + d, NZ) * NX + x, fy) for d in range(1, NZ)]
+    along_x = [(z * NX + lax.rem(x + d, NX), fy) for d in range(1, NX)]
+    along_q = [(fx, lax.rem(fy + d, NQ)) for d in range(1, NQ)]
+    barrier = pltpu.get_barrier_semaphore()
+    for peer in [along_z[d - 1] for d in (4, 3, 5, 2, 6, 1, 7)] + along_x + along_q:
+        pl.semaphore_signal(barrier, inc=1, device_id=peer, device_id_type=MESH)
+
     pairs = [(sky_h, sky), (col_h, col), (row_h, rows), (cnt_h, cnt), (ws_h, ws), (live_h, live), (codes_h, codes), (crd_h, crd), (tab_h, tab)]
     loads = [pltpu.make_async_copy(a, b, load_sem.at[i]) for i, (a, b) in enumerate(pairs)]
     for load in loads:
         load.start()
-
-    along_z = [(lax.rem(z + d, NZ) * NX + x, fy) for d in range(1, NZ)]
-    along_x = [(z * NX + lax.rem(x + d, NX), fy) for d in range(1, NX)]
-    along_q = [(fx, lax.rem(fy + d, NQ)) for d in range(1, NQ)]
-    barrier = pltpu.get_barrier_semaphore()
-    for peer in along_z + along_x + along_q:
-        pl.semaphore_signal(barrier, inc=1, device_id=peer, device_id_type=MESH)
 
     loads[0].wait()
     for j in range(16):
@@ -110,53 +110,57 @@
         tw[d, 0] = cosine
         tw[d, 1] = -sine
 
+    side = iota((8, HALF), 1)
+    high = 2 * (side // 128) + iota((8, HALF), 0) // 4 - 4
+    for r in range(8):
+        mixed = jnp.bitwise_and(r * high * jnp.bitwise_and(side, 127), 7)
+        cosine, sine = cis(mixed.astype(F32) * 0.125)
+        cross[r, 0] = cosine
+        cross[r, 1] = sine
+
     r = iota((128, 64), 0)
     m = iota((128, 64), 1)
-    q, ri, i = jnp.bitwise_and(r, 63) // 8, jnp.bitwise_and(r, 7) // 4, jnp.bitwise_and(r, 3)
+    q, i = jnp.bitwise_and(r, 63) // 8, jnp.bitwise_and(r, 3)
     turn = jnp.bitwise_and((q * (NSKY // NQ) + i) * (rows[fy] + jnp.bitwise_and(m, 31)), NSKY - 1)
-    quarter = ri - (r >= 64).astype(jnp.int32) + (m >= 32).astype(jnp.int32)
+    quarter = (m >= 32).astype(jnp.int32) - (r >= 64).astype(jnp.int32)
     wide = cis(quarter.astype(F32) * 0.25 - turn.astype(F32) * (1.0 / NSKY))[0].astype(BF16)
 
     count = cnt[0, 0]
-    g = iota((32, NV), 0)
-    centre = g - 512
-    middle = g - 16
-
-    def tables(b):
+    g = iota((NV, NV), 0)
+    m = iota((SG0, NV), 0)
+    odd = (jnp.bitwise_and(iota((64, NV), 0), 4) * 32).astype(F32)
+
+    def depth_of(b):
         plane = lax.rem(codes[0, 0, b], count)
         depth = jnp.int32(0)
         for layer in range(8):
             depth = depth + jnp.where(layer <= plane, ws[0, 0, layer], 0)
+        return depth
+
+    def fill(b, carry):
+        depth = depth_of(b)
         u = crd[0, 0, b, 0:1, :]
         v = crd[0, 0, b, 1:2, :]
-        screen = jnp.bitwise_and(depth * middle * middle, 2047).astype(F32) * (1.0 / 2048)
-        wave_real, wave_imag = cis(g.astype(F32) * u + screen)
+        screen = jnp.bitwise_and(depth * (m - 16) * (m - 16), 2047).astype(F32) * (1.0 / 2048)
+        wave_real, wave_imag = cis(m.astype(F32) * u + screen)
         both = jnp.concatenate([wave_real, wave_imag], axis=0).astype(BF16)
-        vtab[b] = jnp.dot(wide, both, preferred_element_type=F32)
-        screen = jnp.bitwise_and(depth * centre * centre, 2047).astype(F32) * (1.0 / 2048)
-        real, imag = cis(g.astype(F32) * v + screen)
-        step = jnp.bitwise_and(depth * (g + 16), 31).astype(F32) * (1.0 / 32)
-        step_real, step_imag = cis(32.0 * v + step)
-        return real, imag, step_real, step_imag
-
-    def fill(b2, carry):
-        blocks = [2 * b2, 2 * b2 + 1]
-        state = [tables(b) for b in blocks]
-        fixed = [s[2:] for s in state]
-
-        def stride(h, values):
-            result = []
-            for b, (real, imag), (sr, si) in zip(blocks, values, fixed):
-                at = pl.ds(pl.multiple_of(32 * h, 32), 32)
-                ker[b, at, 0:NV] = real.astype(BF16)
-                ker[b, at, NV : 2 * NV] = imag.astype(BF16)
-                result.append((real * sr - imag * si, real * si + imag * sr))
-            return tuple(result)
-
-        lax.fori_loop(0, 32, stride, tuple(s[:2] for s in state), unroll=4)
+        turned = jnp.dot(wide, both, preferred_element_type=F32)
+        cosine, sine = cis(256.0 * jnp.broadcast_to(v, (8, NV)))
+        wtab[b, 0] = cosine
+        wtab[b, 1] = sine
+        form[b] = jnp.bitwise_and(depth, 7)
+        cosine, sine = cis(odd * v)
+        vtab[b, 0:64] = turned[:64] * cosine - turned[64:] * sine
+        vtab[b, 64:128] = turned[:64] * sine + turned[64:] * cosine
+        screen = jnp.bitwise_and(depth * g * g, 2047).astype(F32) * (1.0 / 2048)
+        cosine, sine = cis(g.astype(F32) * v + screen)
+        fine[b, 0:NV, 0:NV] = cosine.astype(BF16)
+        fine[b, 0:NV, NV : 2 * NV] = sine.astype(BF16)
+        fine[b, NV : 2 * NV, 0:NV] = (-sine).astype(BF16)
+        fine[b, NV : 2 * NV, NV : 2 * NV] = cosine.astype(BF16)
         return carry
 
-    lax.fori_loop(0, NB // 2, fill, 0)
+    lax.fori_loop(0, NB, fill, 0)
 
     for d in range(1, NZ):
         phase1(d, lax.rem(z + NZ - d, NZ)).wait_recv()
@@ -207,7 +211,14 @@
 
     flat = jnp.concatenate([own[:8], own[8:]], axis=1)
     flat = pltpu.roll(flat, jnp.bitwise_and(SG - jnp.bitwise_and(col[fx], SG - 1), SG - 1), 1)
-    strips[fy] = jnp.concatenate([flat[:, :HALF], flat[:, HALF:]], axis=0).astype(BF16)
+    upper = iota((8, 128), 0) < 4
+    real, imag = [], []
+    for hh in range(4):
+        even, odd_h = flat[:, 256 * hh : 256 * hh + 128], flat[:, 256 * hh + 128 : 256 * hh + 256]
+        real.append(jnp.where(upper, even, pltpu.roll(odd_h, 4, 0)))
+        imag.append(jnp.where(upper, pltpu.roll(even, 4, 0), odd_h))
+    packed = jnp.concatenate([jnp.concatenate(real, axis=1), jnp.concatenate(imag, axis=1)], axis=0)
+    strips[fy] = packed.astype(BF16)
 
     def phase3(d, slot):
         return pltpu.make_async_remote_copy(
@@ -220,21 +231,34 @@
         copy.start()
     for d in range(1, NQ):
         phase3(d, lax.rem(fy + NQ - d, NQ)).wait_recv()
-    wide_strips = strips[...].astype(F32)
-    left_half = wide_strips[:, 0:8, :].reshape(64, HALF)
-    right_half = wide_strips[:, 8:16, :].reshape(64, HALF)
-    lines = jnp.concatenate([left_half, right_half], axis=1).astype(BF16)
+    for hh in range(4):
+        cols = slice(128 * hh, 128 * hh + 128)
+        block = strips[:, :, cols].astype(F32)
+        real, imag = block[:, 0:8, :], block[:, 8:16, :]
+        for r in range(8):
+            cosine, sine = cross[r, 0:1, :, cols], cross[r, 1:2, :, cols]
+            lines[r, 64 * hh : 64 * hh + 64, 0:128] = (real * cosine - imag * sine).reshape(64, 128).astype(BF16)
+            lines[r, 64 * hh : 64 * hh + 64, 128:256] = (real * sine + imag * cosine).reshape(64, 128).astype(BF16)
 
     def degrid(b, carry):
-        prod = jnp.dot(lines, ker[b], preferred_element_type=F32)
-        vr, vi = vtab[b, 0:64, :], vtab[b, 64:128, :]
-        pr, pi = prod[:, :NV], prod[:, NV:]
+        prod = jnp.dot(lines[form[b]], fine[b], preferred_element_type=F32)
+        wr, wi = wtab[b, 0:1], wtab[b, 1:2]
+
+        def tile(hh, lo):
+            return prod[64 * hh : 64 * hh + 64, lo : lo + NV].reshape(8, 8, NV)
+
+        ar, ai = tile(3, 0), tile(3, NV)
+        for hh in (2, 1, 0):
+            ar, ai = ar * wr - ai * wi + tile(hh, 0), ar * wi + ai * wr + tile(hh, NV)
+        vr, vi = vtab[b, 0:64].reshape(8, 8, NV), vtab[b, 64:128].reshape(8, 8, NV)
         scale = jnp.where(b < live[0, 0], 2.0**-18, 0.0)
-        out[0, 0, b, 0:1, :] = jnp.sum(vr * pr - vi * pi, axis=0, keepdims=True) * scale
-        out[0, 0, b, 1:2, :] = jnp.sum(vr * pi + vi * pr, axis=0, keepdims=True) * scale
+        real = jnp.sum(vr * ar - vi * ai, axis=0)
+        imag = jnp.sum(vr * ai + vi * ar, axis=0)
+        out[0, 0, b, 0:1, :] = jnp.sum(real, axis=0, keepdims=True) * scale
+        out[0, 0, b, 1:2, :] = jnp.sum(imag, axis=0, keepdims=True) * scale
         return carry
 
-    lax.fori_loop(0, NB, degrid, 0, unroll=4)
+    lax.fori_loop(0, NB, degrid, 0, unroll=16)
 
     for copy in sent1:
         copy.wait_send()
@@ -271,8 +295,12 @@
             pltpu.VMEM((NX, 16, HALF), BF16),
             pltpu.VMEM((NX, 16, HALF), BF16),
             pltpu.VMEM((NQ, 16, HALF), BF16),
-            pltpu.VMEM((NB, SG, 2 * NV), BF16),
+            pltpu.VMEM((8, 2, 8, HALF), F32),
+            pltpu.VMEM((8, 256, 256), BF16),
+            pltpu.VMEM((NB, 2 * NV, 2 * NV), BF16),
             pltpu.VMEM((NB, 128, NV), F32),
+            pltpu.VMEM((NB, 2, 8, NV), F32),
+            pltpu.SMEM((NB,), jnp.int32),
             dma((9,)), dma((NZ,)), dma((NZ,)), dma((NX,)), dma((NX,)), dma((NQ,)), dma((NQ,)),
         ],
         compiler_params=pltpu.CompilerParams(collective_id=0, has_side_effects=True, vmem_limit_bytes=60 * 2**20),

time: 30.8 us -> 29.2 us (0.948)
  Pallas kernels: 28 us -> 26.4 us
    pallas_call x1, Pallas kernels: 28 us -> 26.4 us  [per_device(): pl.pallas_call(kernel, out_shape=jax.ShapeDtypeStruct((1, 1, NB, 2, NV),...]
where the time goes in v3:
time: 29.2 us; the launch traced here: 29 us
  Pallas kernels  26.4 us (90%)
  local copies, waits for them, and re-layouts  1.32 us (5%)
  between operations  1.3 us (4%)
    pallas_call x1, Pallas kernels, per_device(): pl.pallas_call(kernel, out_shape=jax.ShapeDtypeStruct((1, 1, NB, 2, NV),...  26.4 us
    unnamed x1, local copies, waits for them, and re-layouts  1.32 us

profile of v3, /device:TPU:1, one launch (start us, length us, event | category | flops | bytes accessed | tf_op | source)
XLA Modules:
  0.0 29.0 jit_solution(7286456452923893439)
XLA Ops:
  1.3 26.4 %shard_map.91 = f32[1,1,16,2,128]{4,3,2,1,0:T(2,128)} custom-call(f32[4,2048]{1,0:T(4,128)} %sky_h.1, s32[32]{0:T(128)} %col_h.1, s32[8]{0:T(128)} %row_h.1, s32[1,1]{1,0:T(1,128)S(6)} %copy.11.cnt_h, s32[1,1,8]{2,1,0:T(1,128)} %ws_h.1, s32[1,1]{1,0:T(1,128)S(6)} %copy.12.live_h, s32[1,1,16]{2,1,0:T(1,128)} %codes_h.1, f32[1,1,16,2,128]{4,3,2,1,0:T(2,128)} %crd_h.1, ...), custom_call_target="tpu_custom_call" | custom-call | tf_op jit(solution)/shard_map/pallas_call | solution.py:274
  27.7 1.3 %copy.13 = f32[1,1,16,2,128]{4,3,2,1,0:T(2,128)} copy(f32[1,1,16,2,128]{4,3,2,1,0:T(2,128)} %shard_map.91) | data formatting | bytes 32768

commit v4 on v3

--- a/solution.py
+++ b/solution.py
@@ -16,6 +16,7 @@
 SG0 = 32
 NX = 4
 NZ = 8
+NY = 4
 NQ = 8
 HALF = SG // 2
 F32 = jnp.float32
@@ -55,12 +56,17 @@
 ):
     fx, fy = lax.axis_index("fx"), lax.axis_index("fy")
     z, x = fx // NX, lax.rem(fx, NX)
+    y, core = fy // 2, lax.rem(fy, 2)
 
     along_z = [(lax.rem(z + d, NZ) * NX + x, fy) for d in range(1, NZ)]
-    along_x = [(z * NX + lax.rem(x + d, NX), fy) for d in range(1, NX)]
-    along_q = [(fx, lax.rem(fy + d, NQ)) for d in range(1, NQ)]
+    plane = {
+        (dx, dy): (z * NX + lax.rem(x + dx, NX), lax.rem(y + dy, NY) * 2 + core)
+        for dx in (2, 1, 3, 0) for dy in (2, 1, 3, 0) if dx or dy
+    }
+    other = (fx, y * 2 + 1 - core)
+    peers = [along_z[d - 1] for d in (4, 3, 5, 2, 6, 1, 7)] + list(plane.values()) + [other]
     barrier = pltpu.get_barrier_semaphore()
-    for peer in [along_z[d - 1] for d in (4, 3, 5, 2, 6, 1, 7)] + along_x + along_q:
+    for peer in peers:
         pl.semaphore_signal(barrier, inc=1, device_id=peer, device_id_type=MESH)
 
     pairs = [(sky_h, sky), (col_h, col), (row_h, rows), (cnt_h, cnt), (ws_h, ws), (live_h, live), (codes_h, codes), (crd_h, crd), (tab_h, tab)]
@@ -81,15 +87,16 @@
         halves.append(jnp.concatenate([low, high], axis=0))
     gath[z] = jnp.concatenate(halves, axis=1).astype(BF16)
 
-    pl.semaphore_wait(barrier, len(along_z) + len(along_x) + len(along_q))
-
-    def phase1(d, slot):
+    pl.semaphore_wait(barrier, len(peers))
+
+    def phase1(slot, there):
         return pltpu.make_async_remote_copy(
-            src_ref=gath.at[slot], dst_ref=gath.at[slot], send_sem=send1.at[d], recv_sem=recv1.at[d],
-            device_id=along_z[d - 1], device_id_type=MESH,
+            src_ref=gath.at[slot], dst_ref=gath.at[slot], send_sem=send1.at[there], recv_sem=recv1.at[slot],
+            device_id=(there * NX + x, fy), device_id_type=MESH,
         )
 
-    sent1 = [phase1(d, z) for d in (4, 3, 5, 2, 6, 1, 7)]
+    others_z = [j + (z <= j).astype(jnp.int32) for j in range(NZ - 1)]
+    sent1 = [phase1(z, there) for there in others_z]
     for copy in sent1:
         copy.start()
     for load in loads[1:]:
@@ -102,7 +109,7 @@
         return off + jnp.bitwise_and(kappa - off, SG - 1)
 
     for d in range(NX):
-        k = wave(col[z * NX + lax.rem(x + d, NX)])
+        k = wave(col[z * NX + d])
         cosine, sine = cis(jnp.bitwise_and(k * 8, NSKY - 1).astype(F32) * (1.0 / NSKY))
         w8[d, 0] = cosine
         w8[d, 1] = -sine
@@ -120,7 +127,8 @@
 
     r = iota((128, 64), 0)
     m = iota((128, 64), 1)
-    q, i = jnp.bitwise_and(r, 63) // 8, jnp.bitwise_and(r, 3)
+    q = 2 * (jnp.bitwise_and(r, 31) // 8) + jnp.bitwise_and(r, 63) // 32
+    i = jnp.bitwise_and(r, 3)
     turn = jnp.bitwise_and((q * (NSKY // NQ) + i) * (rows[fy] + jnp.bitwise_and(m, 31)), NSKY - 1)
     quarter = (m >= 32).astype(jnp.int32) - (r >= 64).astype(jnp.int32)
     wide = cis(quarter.astype(F32) * 0.25 - turn.astype(F32) * (1.0 / NSKY))[0].astype(BF16)
@@ -162,8 +170,8 @@
 
     lax.fori_loop(0, NB, fill, 0)
 
-    for d in range(1, NZ):
-        phase1(d, lax.rem(z + NZ - d, NZ)).wait_recv()
+    for there in others_z:
+        phase1(there, there).wait_recv()
 
     sky_t = gath[...].reshape(NZ * 32, 256)
     spec[...] = lax.dot_general(sky_t, tab[...], (((0,), (0,)), ((), ())), preferred_element_type=F32)
@@ -173,14 +181,15 @@
         (pick_col // 16 == jnp.bitwise_and(pick_row, 3)) & (jnp.bitwise_and(pick_col // 8, 1) == pick_row // 4), 1.0, 0.0
     ).astype(BF16)
 
-    def phase2(d):
+    def phase2(slot, to_x, to_y):
         return pltpu.make_async_remote_copy(
-            src_ref=part.at[d], dst_ref=got.at[d], send_sem=send2.at[d], recv_sem=recv2.at[d],
-            device_id=along_x[d - 1], device_id_type=MESH,
+            src_ref=part.at[to_x], dst_ref=got.at[slot], send_sem=send2.at[NY * to_x + to_y], recv_sem=recv2.at[slot],
+            device_id=(z * NX + to_x, to_y * 2 + core), device_id_type=MESH,
         )
 
-    own = None
-    for d in (2, 1, 3, 0):
+    here = NY * x + y
+    others_xy = [j + (here <= j).astype(jnp.int32) for j in range(NX * NY - 1)]
+    for d in range(NX):
         def facet_row(x0, carry):
             for lo in (0, HALF):
                 cols = slice(lo, lo + HALF)
@@ -200,40 +209,47 @@
         lax.fori_loop(0, 4, facet_row, 0)
         strip = jnp.dot(pick, ybuf[d], preferred_element_type=F32)
         packed = jnp.concatenate([strip[:, :HALF], strip[:, HALF:]], axis=0)
-        if d:
-            part[d] = packed.astype(BF16)
-            phase2(d).start()
-        else:
-            own = packed
-    for d in (1, 3, 2):
-        phase2(d).wait_recv()
-        own = own + got[d].astype(F32)
-
-    flat = jnp.concatenate([own[:8], own[8:]], axis=1)
-    flat = pltpu.roll(flat, jnp.bitwise_and(SG - jnp.bitwise_and(col[fx], SG - 1), SG - 1), 1)
+        part[d] = packed.astype(BF16)
+        for to_y in range(NY):
+            @pl.when(jnp.logical_or(x != d, y != to_y))
+            def send():
+                phase2(here, d, to_y).start()
+
+    got[here] = part[x]
+    for there in others_xy:
+        phase2(there, there // NY, lax.rem(there, NY)).wait_recv()
+
+    totals = []
+    for dy in range(NY):
+        total = got[dy].astype(F32)
+        for dx in range(1, NX):
+            total = total + got[NY * dx + dy].astype(F32)
+        totals.append(jnp.concatenate([total[:8], total[8:]], axis=1))
+    shift = jnp.bitwise_and(SG - jnp.bitwise_and(col[fx], SG - 1), SG - 1)
+    ordered = pltpu.roll(jnp.concatenate(totals, axis=0), shift, 1)
     upper = iota((8, 128), 0) < 4
-    real, imag = [], []
-    for hh in range(4):
-        even, odd_h = flat[:, 256 * hh : 256 * hh + 128], flat[:, 256 * hh + 128 : 256 * hh + 256]
-        real.append(jnp.where(upper, even, pltpu.roll(odd_h, 4, 0)))
-        imag.append(jnp.where(upper, pltpu.roll(even, 4, 0), odd_h))
-    packed = jnp.concatenate([jnp.concatenate(real, axis=1), jnp.concatenate(imag, axis=1)], axis=0)
-    strips[fy] = packed.astype(BF16)
-
-    def phase3(d, slot):
+    for dy in range(NY):
+        flat = ordered[8 * dy : 8 * dy + 8]
+        real, imag = [], []
+        for hh in range(4):
+            even, odd_h = flat[:, 256 * hh : 256 * hh + 128], flat[:, 256 * hh + 128 : 256 * hh + 256]
+            real.append(jnp.where(upper, even, pltpu.roll(odd_h, 4, 0)))
+            imag.append(jnp.where(upper, pltpu.roll(even, 4, 0), odd_h))
+        packed = jnp.concatenate([jnp.concatenate(real, axis=1), jnp.concatenate(imag, axis=1)], axis=0)
+        strips[core, dy] = packed.astype(BF16)
+
+    def phase3(slot):
         return pltpu.make_async_remote_copy(
-            src_ref=strips.at[slot], dst_ref=strips.at[slot], send_sem=send3.at[d], recv_sem=recv3.at[d],
-            device_id=along_q[d - 1], device_id_type=MESH,
+            src_ref=strips.at[slot], dst_ref=strips.at[slot], send_sem=send3, recv_sem=recv3,
+            device_id=other, device_id_type=MESH,
         )
 
-    sent3 = [phase3(d, fy) for d in (4, 3, 5, 2, 6, 1, 7)]
-    for copy in sent3:
-        copy.start()
-    for d in range(1, NQ):
-        phase3(d, lax.rem(fy + NQ - d, NQ)).wait_recv()
+    sent3 = phase3(core)
+    sent3.start()
+    phase3(1 - core).wait_recv()
     for hh in range(4):
         cols = slice(128 * hh, 128 * hh + 128)
-        block = strips[:, :, cols].astype(F32)
+        block = strips[:, :, :, cols].astype(F32).reshape(NQ, 16, 128)
         real, imag = block[:, 0:8, :], block[:, 8:16, :]
         for r in range(8):
             cosine, sine = cross[r, 0:1, :, cols], cross[r, 1:2, :, cols]
@@ -262,10 +278,9 @@
 
     for copy in sent1:
         copy.wait_send()
-    for d in (2, 1, 3):
-        phase2(d).wait_send()
-    for copy in sent3:
-        copy.wait_send()
+    for there in others_xy:
+        phase2(here, there // NY, lax.rem(there, NY)).wait_send()
+    sent3.wait_send()
 
 
 def per_device(sky, col, rows, cnt, ws, live, codes, crd):
@@ -293,15 +308,15 @@
             pltpu.VMEM((NX, 2, 8, SG), F32),
             pltpu.VMEM((NX, 64, SG), BF16),
             pltpu.VMEM((NX, 16, HALF), BF16),
-            pltpu.VMEM((NX, 16, HALF), BF16),
-            pltpu.VMEM((NQ, 16, HALF), BF16),
+            pltpu.VMEM((NX * NY, 16, HALF), BF16),
+            pltpu.VMEM((2, NY, 16, HALF), BF16),
             pltpu.VMEM((8, 2, 8, HALF), F32),
             pltpu.VMEM((8, 256, 256), BF16),
             pltpu.VMEM((NB, 2 * NV, 2 * NV), BF16),
             pltpu.VMEM((NB, 128, NV), F32),
             pltpu.VMEM((NB, 2, 8, NV), F32),
             pltpu.SMEM((NB,), jnp.int32),
-            dma((9,)), dma((NZ,)), dma((NZ,)), dma((NX,)), dma((NX,)), dma((NQ,)), dma((NQ,)),
+            dma((9,)), dma((NZ,)), dma((NZ,)), dma((NX * NY,)), dma((NX * NY,)), dma, dma,
         ],
         compiler_params=pltpu.CompilerParams(collective_id=0, has_side_effects=True, vmem_limit_bytes=60 * 2**20),
     )(sky, col, rows, cnt, ws, live, codes, crd, jnp.asarray(dft_table()))

time: 29.2 us -> 28.2 us (0.966)
  Pallas kernels: 26.4 us -> 25.4 us
    pallas_call x1, Pallas kernels: 26.4 us -> 25.4 us  [per_device(): pl.pallas_call(kernel, out_shape=jax.ShapeDtypeStruct((1, 1, NB, 2, NV),...]
where the time goes in v4:
time: 28.2 us; the launch traced here: 28 us
  Pallas kernels  25.4 us (90%)
  local copies, waits for them, and re-layouts  1.32 us (5%)
  between operations  1.3 us (5%)
    pallas_call x1, Pallas kernels, per_device(): pl.pallas_call(kernel, out_shape=jax.ShapeDtypeStruct((1, 1, NB, 2, NV),...  25.4 us
    unnamed x1, local copies, waits for them, and re-layouts  1.32 us

profile of v4, /device:TPU:1, one launch (start us, length us, event | category | flops | bytes accessed | tf_op | source)
XLA Modules:
  0.0 28.0 jit_solution(18026358805158867727)
XLA Ops:
  1.3 25.4 %shard_map.91 = f32[1,1,16,2,128]{4,3,2,1,0:T(2,128)} custom-call(f32[4,2048]{1,0:T(4,128)} %sky_h.1, s32[32]{0:T(128)} %col_h.1, s32[8]{0:T(128)} %row_h.1, s32[1,1]{1,0:T(1,128)S(6)} %copy.11.cnt_h, s32[1,1,8]{2,1,0:T(1,128)} %ws_h.1, s32[1,1]{1,0:T(1,128)S(6)} %copy.12.live_h, s32[1,1,16]{2,1,0:T(1,128)} %codes_h.1, f32[1,1,16,2,128]{4,3,2,1,0:T(2,128)} %crd_h.1, ...), custom_call_target="tpu_custom_call" | custom-call | tf_op jit(solution)/shard_map/pallas_call | solution.py:289
  26.7 1.3 %copy.13 = f32[1,1,16,2,128]{4,3,2,1,0:T(2,128)} copy(f32[1,1,16,2,128]{4,3,2,1,0:T(2,128)} %shard_map.91) | data formatting | bytes 32768

commit v5 on v4

--- a/solution.py
+++ b/solution.py
@@ -51,7 +51,7 @@
 
 def kernel(
     sky_h, col_h, row_h, cnt_h, ws_h, live_h, codes_h, crd_h, tab_h, out,
-    sky, tmp, tab, crd, col, rows, cnt, ws, live, codes, gath, spec, w8, tw, ybuf, part, got, strips, cross, lines, fine, vtab, wtab, form,
+    sky, tmp, tab, crd, col, rows, cnt, ws, live, codes, gath, spec, w8, tw, ybuf, part, got, strips, cross, lines, fine, vtab, wtab, form, acc,
     load_sem, send1, recv1, send2, recv2, send3, recv3,
 ):
     fx, fy = lax.axis_index("fx"), lax.axis_index("fy")
@@ -127,7 +127,7 @@
 
     r = iota((128, 64), 0)
     m = iota((128, 64), 1)
-    q = 2 * (jnp.bitwise_and(r, 31) // 8) + jnp.bitwise_and(r, 63) // 32
+    q = 2 * (jnp.bitwise_and(r, 31) // 8) + jnp.where(jnp.bitwise_and(r, 32) == 0, core, 1 - core)
     i = jnp.bitwise_and(r, 3)
     turn = jnp.bitwise_and((q * (NSKY // NQ) + i) * (rows[fy] + jnp.bitwise_and(m, 31)), NSKY - 1)
     quarter = (m >= 32).astype(jnp.int32) - (r >= 64).astype(jnp.int32)
@@ -246,35 +246,48 @@
 
     sent3 = phase3(core)
     sent3.start()
-    phase3(1 - core).wait_recv()
-    for hh in range(4):
-        cols = slice(128 * hh, 128 * hh + 128)
-        block = strips[:, :, :, cols].astype(F32).reshape(NQ, 16, 128)
-        real, imag = block[:, 0:8, :], block[:, 8:16, :]
-        for r in range(8):
-            cosine, sine = cross[r, 0:1, :, cols], cross[r, 1:2, :, cols]
-            lines[r, 64 * hh : 64 * hh + 64, 0:128] = (real * cosine - imag * sine).reshape(64, 128).astype(BF16)
-            lines[r, 64 * hh : 64 * hh + 64, 128:256] = (real * sine + imag * cosine).reshape(64, 128).astype(BF16)
-
-    def degrid(b, carry):
-        prod = jnp.dot(lines[form[b]], fine[b], preferred_element_type=F32)
+
+    def turn_lines(where, half):
+        for hh in range(4):
+            cols = slice(128 * hh, 128 * hh + 128)
+            rows_at = slice(32 * hh, 32 * hh + 32)
+            block = strips[where, :, :, cols].astype(F32)
+            real, imag = block[:, 0:8, :], block[:, 8:16, :]
+            for r in range(8):
+                cosine, sine = cross[r, 0:1, :, cols], cross[r, 1:2, :, cols]
+                lines[r, half, rows_at, 0:128] = (real * cosine - imag * sine).reshape(32, 128).astype(BF16)
+                lines[r, half, rows_at, 128:256] = (real * sine + imag * cosine).reshape(32, 128).astype(BF16)
+
+    def gridded(b, half):
+        prod = jnp.dot(lines[form[b], half], fine[b], preferred_element_type=F32)
         wr, wi = wtab[b, 0:1], wtab[b, 1:2]
 
         def tile(hh, lo):
-            return prod[64 * hh : 64 * hh + 64, lo : lo + NV].reshape(8, 8, NV)
+            return prod[32 * hh : 32 * hh + 32, lo : lo + NV].reshape(4, 8, NV)
 
         ar, ai = tile(3, 0), tile(3, NV)
         for hh in (2, 1, 0):
             ar, ai = ar * wr - ai * wi + tile(hh, 0), ar * wi + ai * wr + tile(hh, NV)
-        vr, vi = vtab[b, 0:64].reshape(8, 8, NV), vtab[b, 64:128].reshape(8, 8, NV)
+        at = 32 * half
+        vr, vi = vtab[b, at : at + 32].reshape(4, 8, NV), vtab[b, 64 + at : 96 + at].reshape(4, 8, NV)
+        return jnp.sum(vr * ar - vi * ai, axis=0), jnp.sum(vr * ai + vi * ar, axis=0)
+
+    def own_rows(b, carry):
+        acc[b, 0], acc[b, 1] = gridded(b, 0)
+        return carry
+
+    def other_rows(b, carry):
+        real, imag = gridded(b, 1)
         scale = jnp.where(b < live[0, 0], 2.0**-18, 0.0)
-        real = jnp.sum(vr * ar - vi * ai, axis=0)
-        imag = jnp.sum(vr * ai + vi * ar, axis=0)
-        out[0, 0, b, 0:1, :] = jnp.sum(real, axis=0, keepdims=True) * scale
-        out[0, 0, b, 1:2, :] = jnp.sum(imag, axis=0, keepdims=True) * scale
+        out[0, 0, b, 0:1, :] = jnp.sum(acc[b, 0] + real, axis=0, keepdims=True) * scale
+        out[0, 0, b, 1:2, :] = jnp.sum(acc[b, 1] + imag, axis=0, keepdims=True) * scale
         return carry
 
-    lax.fori_loop(0, NB, degrid, 0, unroll=16)
+    turn_lines(core, 0)
+    lax.fori_loop(0, NB, own_rows, 0, unroll=16)
+    phase3(1 - core).wait_recv()
+    turn_lines(1 - core, 1)
+    lax.fori_loop(0, NB, other_rows, 0, unroll=16)
 
     for copy in sent1:
         copy.wait_send()
@@ -311,11 +324,12 @@
             pltpu.VMEM((NX * NY, 16, HALF), BF16),
             pltpu.VMEM((2, NY, 16, HALF), BF16),
             pltpu.VMEM((8, 2, 8, HALF), F32),
-            pltpu.VMEM((8, 256, 256), BF16),
+            pltpu.VMEM((8, 2, 128, 256), BF16),
             pltpu.VMEM((NB, 2 * NV, 2 * NV), BF16),
             pltpu.VMEM((NB, 128, NV), F32),
             pltpu.VMEM((NB, 2, 8, NV), F32),
             pltpu.SMEM((NB,), jnp.int32),
+            pltpu.VMEM((NB, 2, 8, NV), F32),
             dma((9,)), dma((NZ,)), dma((NZ,)), dma((NX * NY,)), dma((NX * NY,)), dma, dma,
         ],
         compiler_params=pltpu.CompilerParams(collective_id=0, has_side_effects=True, vmem_limit_bytes=60 * 2**20),

time: 28.2 us -> 27.7 us (0.982)
  Pallas kernels: 25.4 us -> 24.9 us
    pallas_call x1, Pallas kernels: 25.4 us -> 24.9 us  [per_device(): pl.pallas_call(kernel, out_shape=jax.ShapeDtypeStruct((1, 1, NB, 2, NV),...]
where the time goes in v5:
time: 27.7 us; the launch traced here: 27.5 us
  Pallas kernels  24.9 us (90%)
  local copies, waits for them, and re-layouts  1.32 us (5%)
  between operations  1.3 us (5%)
    pallas_call x1, Pallas kernels, per_device(): pl.pallas_call(kernel, out_shape=jax.ShapeDtypeStruct((1, 1, NB, 2, NV),...  24.9 us
    unnamed x1, local copies, waits for them, and re-layouts  1.32 us

profile of v5, /device:TPU:1, one launch (start us, length us, event | category | flops | bytes accessed | tf_op | source)
XLA Modules:
  0.0 27.5 jit_solution(14560873155736301874)
XLA Ops:
  1.3 24.9 %shard_map.91 = f32[1,1,16,2,128]{4,3,2,1,0:T(2,128)} custom-call(f32[4,2048]{1,0:T(4,128)} %sky_h.1, s32[32]{0:T(128)} %col_h.1, s32[8]{0:T(128)} %row_h.1, s32[1,1]{1,0:T(1,128)S(6)} %copy.11.cnt_h, s32[1,1,8]{2,1,0:T(1,128)} %ws_h.1, s32[1,1]{1,0:T(1,128)S(6)} %copy.12.live_h, s32[1,1,16]{2,1,0:T(1,128)} %codes_h.1, f32[1,1,16,2,128]{4,3,2,1,0:T(2,128)} %crd_h.1, ...), custom_call_target="tpu_custom_call" | custom-call | tf_op jit(solution)/shard_map/pallas_call | solution.py:302
  26.2 1.3 %copy.13 = f32[1,1,16,2,128]{4,3,2,1,0:T(2,128)} copy(f32[1,1,16,2,128]{4,3,2,1,0:T(2,128)} %shard_map.91) | data formatting | bytes 32768

commit v6 on v5

--- a/solution.py
+++ b/solution.py
@@ -87,18 +87,6 @@
         halves.append(jnp.concatenate([low, high], axis=0))
     gath[z] = jnp.concatenate(halves, axis=1).astype(BF16)
 
-    pl.semaphore_wait(barrier, len(peers))
-
-    def phase1(slot, there):
-        return pltpu.make_async_remote_copy(
-            src_ref=gath.at[slot], dst_ref=gath.at[slot], send_sem=send1.at[there], recv_sem=recv1.at[slot],
-            device_id=(there * NX + x, fy), device_id_type=MESH,
-        )
-
-    others_z = [j + (z <= j).astype(jnp.int32) for j in range(NZ - 1)]
-    sent1 = [phase1(z, there) for there in others_z]
-    for copy in sent1:
-        copy.start()
     for load in loads[1:]:
         load.wait()
 
@@ -117,6 +105,18 @@
         tw[d, 0] = cosine
         tw[d, 1] = -sine
 
+    pl.semaphore_wait(barrier, len(peers))
+
+    def phase1(slot, there):
+        return pltpu.make_async_remote_copy(
+            src_ref=gath.at[slot], dst_ref=gath.at[slot], send_sem=send1.at[there], recv_sem=recv1.at[slot],
+            device_id=(there * NX + x, fy), device_id_type=MESH,
+        )
+
+    others_z = [j + (z <= j).astype(jnp.int32) for j in range(NZ - 1)]
+    sent1 = [phase1(z, there) for there in others_z]
+    for copy in sent1:
+        copy.start()
     side = iota((8, HALF), 1)
     high = 2 * (side // 128) + iota((8, HALF), 0) // 4 - 4
     for r in range(8):
@@ -168,13 +168,16 @@
         fine[b, NV : 2 * NV, NV : 2 * NV] = cosine.astype(BF16)
         return carry
 
-    lax.fori_loop(0, NB, fill, 0)
+    lax.fori_loop(0, 8, fill, 0)
 
     for there in others_z:
         phase1(there, there).wait_recv()
 
     sky_t = gath[...].reshape(NZ * 32, 256)
-    spec[...] = lax.dot_general(sky_t, tab[...], (((0,), (0,)), ((), ())), preferred_element_type=F32)
+    for lo in (0, HALF):
+        for plus in (0, SG):
+            cols = slice(lo + plus, lo + plus + HALF)
+            spec[:, cols] = lax.dot_general(sky_t, tab[:, cols], (((0,), (0,)), ((), ())), preferred_element_type=F32)
     pick_row = iota((8, 64), 0)
     pick_col = iota((8, 64), 1)
     pick = jnp.where(
@@ -190,23 +193,25 @@
     here = NY * x + y
     others_xy = [j + (here <= j).astype(jnp.int32) for j in range(NX * NY - 1)]
     for d in range(NX):
-        def facet_row(x0, carry):
-            for lo in (0, HALF):
+        def facet_row(step, carry):
+            x0, lo = step % 4, HALF * (step // 4)
+            for lo in (lo,):
                 cols = slice(lo, lo + HALF)
                 wr, wi = w8[d, 0, :, cols], w8[d, 1, :, cols]
 
                 def at(c1, plus):
-                    return spec[pl.ds(pl.multiple_of(x0 * 64 + 8 * c1, 8), 8), lo + plus : lo + plus + HALF]
+                    return spec[x0 * 64 + 8 * c1 : x0 * 64 + 8 * c1 + 8, lo + plus : lo + plus + HALF]
 
                 ar, ai = at(7, 0), at(7, SG)
                 for c1 in range(6, -1, -1):
                     ar, ai = ar * wr - ai * wi + at(c1, 0), ar * wi + ai * wr + at(c1, SG)
                 tr, ti = tw[d, 0, :, cols], tw[d, 1, :, cols]
                 both = jnp.concatenate([ar * tr - ai * ti, ar * ti + ai * tr], axis=0)
-                ybuf[d, pl.ds(pl.multiple_of(x0 * 16, 16), 16), cols] = both.astype(BF16)
+                ybuf[d, 16 * x0 : 16 * x0 + 16, cols] = both.astype(BF16)
             return carry
 
-        lax.fori_loop(0, 4, facet_row, 0)
+        for step in range(8):
+            facet_row(step, 0)
         strip = jnp.dot(pick, ybuf[d], preferred_element_type=F32)
         packed = jnp.concatenate([strip[:, :HALF], strip[:, HALF:]], axis=0)
         part[d] = packed.astype(BF16)
@@ -216,6 +221,7 @@
                 phase2(here, d, to_y).start()
 
     got[here] = part[x]
+    lax.fori_loop(8, NB, fill, 0)
     for there in others_xy:
         phase2(there, there // NY, lax.rem(there, NY)).wait_recv()
 

time: 27.7 us -> 26.7 us (0.964)
  Pallas kernels: 24.9 us -> 23.9 us
    pallas_call x1, Pallas kernels: 24.9 us -> 23.9 us  [per_device(): pl.pallas_call(kernel, out_shape=jax.ShapeDtypeStruct((1, 1, NB, 2, NV),...]
where the time goes in v6:
time: 26.7 us; the launch traced here: 26.6 us
  Pallas kernels  23.9 us (90%)
  local copies, waits for them, and re-layouts  1.32 us (5%)
  between operations  1.3 us (5%)
    pallas_call x1, Pallas kernels, per_device(): pl.pallas_call(kernel, out_shape=jax.ShapeDtypeStruct((1, 1, NB, 2, NV),...  23.9 us
    unnamed x1, local copies, waits for them, and re-layouts  1.32 us

profile of v6, /device:TPU:1, one launch (start us, length us, event | category | flops | bytes accessed | tf_op | source)
XLA Modules:
  0.0 26.6 jit_solution(17974651107270442010)
XLA Ops:
  1.3 23.9 %shard_map.91 = f32[1,1,16,2,128]{4,3,2,1,0:T(2,128)} custom-call(f32[4,2048]{1,0:T(4,128)} %sky_h.1, s32[32]{0:T(128)} %col_h.1, s32[8]{0:T(128)} %row_h.1, s32[1,1]{1,0:T(1,128)S(6)} %copy.11.cnt_h, s32[1,1,8]{2,1,0:T(1,128)} %ws_h.1, s32[1,1]{1,0:T(1,128)S(6)} %copy.12.live_h, s32[1,1,16]{2,1,0:T(1,128)} %codes_h.1, f32[1,1,16,2,128]{4,3,2,1,0:T(2,128)} %crd_h.1, ...), custom_call_target="tpu_custom_call" | custom-call | tf_op jit(solution)/shard_map/pallas_call | solution.py:308
  25.2 1.3 %copy.13 = f32[1,1,16,2,128]{4,3,2,1,0:T(2,128)} copy(f32[1,1,16,2,128]{4,3,2,1,0:T(2,128)} %shard_map.91) | data formatting | bytes 32768

commit v7 on v6

--- a/solution.py
+++ b/solution.py
@@ -136,7 +136,7 @@
     count = cnt[0, 0]
     g = iota((NV, NV), 0)
     m = iota((SG0, NV), 0)
-    odd = (jnp.bitwise_and(iota((64, NV), 0), 4) * 32).astype(F32)
+    odd = (jnp.bitwise_and(iota((8, NV), 0), 4) * 32).astype(F32)
 
     def depth_of(b):
         plane = lax.rem(codes[0, 0, b], count)
@@ -158,8 +158,9 @@
         wtab[b, 1] = sine
         form[b] = jnp.bitwise_and(depth, 7)
         cosine, sine = cis(odd * v)
-        vtab[b, 0:64] = turned[:64] * cosine - turned[64:] * sine
-        vtab[b, 64:128] = turned[:64] * sine + turned[64:] * cosine
+        real, imag = turned[:64].reshape(8, 8, NV), turned[64:].reshape(8, 8, NV)
+        vtab[b, 0:64] = (real * cosine[None] - imag * sine[None]).reshape(64, NV)
+        vtab[b, 64:128] = (real * sine[None] + imag * cosine[None]).reshape(64, NV)
         screen = jnp.bitwise_and(depth * g * g, 2047).astype(F32) * (1.0 / 2048)
         cosine, sine = cis(g.astype(F32) * v + screen)
         fine[b, 0:NV, 0:NV] = cosine.astype(BF16)

time: 26.7 us -> 26.7 us (level)
  no operation moved by 1% of the time
where the time goes in v7:
time: 26.7 us; the launch traced here: 26.6 us
  Pallas kernels  23.9 us (90%)
  local copies, waits for them, and re-layouts  1.32 us (5%)
  between operations  1.3 us (5%)
    pallas_call x1, Pallas kernels, per_device(): pl.pallas_call(kernel, out_shape=jax.ShapeDtypeStruct((1, 1, NB, 2, NV),...  23.9 us
    unnamed x1, local copies, waits for them, and re-layouts  1.32 us

profile of v7, /device:TPU:1, one launch (start us, length us, event | category | flops | bytes accessed | tf_op | source)
XLA Modules:
  0.0 26.6 jit_solution(12103126126406877206)
XLA Ops:
  1.3 23.9 %shard_map.91 = f32[1,1,16,2,128]{4,3,2,1,0:T(2,128)} custom-call(f32[4,2048]{1,0:T(4,128)} %sky_h.1, s32[32]{0:T(128)} %col_h.1, s32[8]{0:T(128)} %row_h.1, s32[1,1]{1,0:T(1,128)S(6)} %copy.11.cnt_h, s32[1,1,8]{2,1,0:T(1,128)} %ws_h.1, s32[1,1]{1,0:T(1,128)S(6)} %copy.12.live_h, s32[1,1,16]{2,1,0:T(1,128)} %codes_h.1, f32[1,1,16,2,128]{4,3,2,1,0:T(2,128)} %crd_h.1, ...), custom_call_target="tpu_custom_call" | custom-call | tf_op jit(solution)/shard_map/pallas_call | solution.py:309
  25.2 1.3 %copy.13 = f32[1,1,16,2,128]{4,3,2,1,0:T(2,128)} copy(f32[1,1,16,2,128]{4,3,2,1,0:T(2,128)} %shard_map.91) | data formatting | bytes 32768
